TPU v7x, 256 devices: a whole 4x4x8 slice. The times are simulated.
256 devices in a mesh: angle: 8 (over x_hi, y), tile: 16 (over z, core), layer: 2 (over x_lo).
Axes of the slice: x: 4 (x_hi: 2, x_lo: 2; x = x_hi * 2 + x_lo), y: 4, z: 8, core: 2. Of those that a mesh axis runs over, the one named last changes fastest.
Arguments:
- frames: bfloat16 [2, 1024, 384, 2048], P('layer', 'angle', 'tile'), may hold values from 0.0625 to 8, as said below
- exponents: int32 [2, 1024, 384, 16], P('layer', 'angle', 'tile'), may hold values from -1 to 1
- valid_mask: int32 [2, 384, 2048], P('layer', 'tile', 'angle'), may hold values 0 or 1
Outputs:
- orientation: float32 [2, 2, 384, 2048], P(None, 'layer', 'tile', 'angle')
- spread: float32 [3, 2, 384, 2048], P(None, 'layer', 'tile', 'angle')
- nye_tensor: float32 [7, 2, 384, 2048], P(None, 'layer', 'tile', 'angle')
Inputs may be any that keep to these rules, and one draw needn't show every extreme that they name: `frames`: positive intensities.
All inputs are finite; a program needn't handle non-finite values. No bound on the sum of `valid_mask` on one device may be relied on, other than what follows from the above.
Results may differ from a plain program's by a relative error of at most 0.0003.
Values sent between devices are 32-bit elements; how exact they have to be, the bound alone decides.
A program may use at most 128 MiB of HBM per device.

v0:
```python
import jax
import jax.numpy as jnp
from jax import lax
from jax.sharding import PartitionSpec as P

NPHI = 32
NCHI = 32


layer_pitch = 2.0


def padded_2(cells, sides, width):
    for axis, dim in sides:
        count = lax.axis_size(axis)
        ends = count - 1
        head = lax.slice_in_dim(cells, 0, width, axis=dim)
        tail = lax.slice_in_dim(cells, cells.shape[dim] - width, cells.shape[dim], axis=dim)
        cells = jnp.concatenate(
            [
                lax.ppermute(tail, axis, [(i, (i + 1) % count) for i in range(ends)]),
                cells,
                lax.ppermute(head, axis, [((i + 1) % count, i) for i in range(ends)]),
            ],
            axis=dim,
        )
    return cells


def angle_table(first_angle, count_angles):
    position = first_angle + jnp.arange(count_angles, dtype=jnp.int32)
    phi_index = (position // NCHI).astype(jnp.float32)
    chi_index = (position % NCHI).astype(jnp.float32)
    phi_coord = (phi_index - 0.5 * (NPHI - 1)) / (0.5 * NPHI)
    chi_coord = (chi_index - 0.5 * (NCHI - 1)) / (0.5 * NCHI)
    constant = jnp.ones_like(phi_coord)
    return jnp.stack(
        [
            constant,
            phi_coord,
            chi_coord,
            phi_coord * phi_coord,
            chi_coord * chi_coord,
            phi_coord * chi_coord,
        ]
    ).astype(jnp.bfloat16)


def intensity_of(frames, exponents):
    layers_here, angles_here, rows_here, columns = frames.shape
    blocks = exponents.shape[3]
    factor = jnp.exp2(exponents.astype(jnp.float32)).astype(jnp.bfloat16)
    scaled = (
        frames.reshape(layers_here, angles_here, rows_here, blocks, columns // blocks)
        * factor[..., None]
    )
    return scaled.reshape(layers_here, angles_here, rows_here * columns)


def orientation_of(moments):
    zeroth = moments[0]
    return jnp.stack([moments[1] / zeroth, moments[2] / zeroth])


def spread_of(moments, orient):
    zeroth = moments[0]
    return jnp.stack(
        [
            moments[3] / zeroth - orient[0] * orient[0],
            moments[4] / zeroth - orient[1] * orient[1],
            moments[5] / zeroth - orient[0] * orient[1],
        ]
    )


def nye_of(padded):
    along_x = 0.5 * (padded[:, 1:-1, 1:-1, 2:] - padded[:, 1:-1, 1:-1, :-2])
    along_y = 0.5 * (padded[:, 1:-1, 2:, 1:-1] - padded[:, 1:-1, :-2, 1:-1])
    along_z = 0.5 / layer_pitch * (padded[:, 2:, 1:-1, 1:-1] - padded[:, :-2, 1:-1, 1:-1])
    trace_sum = along_x[0] + along_y[1]
    return jnp.stack(
        [-along_y[1], -along_x[0], -trace_sum, along_x[1], along_y[0], along_z[0], along_z[1]]
    )


def on_device(frames, exponents, valid_mask):
    layers_here, angles_here, rows_here, columns = frames.shape
    intensity = intensity_of(frames, exponents)
    angle_weights = angle_table(lax.axis_index("angle") * angles_here, angles_here)
    partial_value = jnp.einsum(
        "ma,lax->mlx", angle_weights, intensity, preferred_element_type=jnp.float32
    )
    partial_value = partial_value.reshape(6, layers_here, rows_here, columns)
    own_columns = columns // lax.axis_size("angle")
    offset = lax.axis_index("angle") * own_columns
    summed_all = lax.psum(partial_value, "angle")
    orient_all = orientation_of(summed_all)
    margined = jnp.pad(orient_all, ((0, 0), (0, 0), (0, 0), (1, 1)))
    window = lax.dynamic_slice_in_dim(margined, offset, own_columns + 2, 3)
    padded = padded_2(window, (("tile", 2), ("layer", 1)), 1)
    moments = lax.dynamic_slice_in_dim(summed_all, offset, own_columns, 3)
    orient = window[:, :, :, 1:-1]
    mask_float = valid_mask.astype(jnp.float32)
    spread = spread_of(moments, orient) * mask_float
    nye_tensor = nye_of(padded) * mask_float
    return (orient * mask_float, spread, nye_tensor)


def solution(mesh):
    in_specs = (
        P("layer", "angle", "tile", None),
        P("layer", "angle", "tile", None),
        P("layer", "tile", "angle"),
    )
    out_specs = (
        P(None, "layer", "tile", "angle"),
        P(None, "layer", "tile", "angle"),
        P(None, "layer", "tile", "angle"),
    )
    return jax.shard_map(
        on_device, mesh=mesh, in_specs=in_specs, out_specs=out_specs, check_vma=False
    )
```

profile of v0, /device:TPU:100, one launch (start us, length us, event | category | flops | bytes accessed | tf_op | source)
XLA Modules:
  0.0 216.0 jit_solution(16204124210433963389)
XLA Ops:
  7.2 0.0 all-reduce.3.cloned.1.call-start
  7.3 0.0 copy-start.1
  7.3 14.6 %copy.11 = bf16[16,8,24,2048]{3,1,2,0:T(8,128)(2,1)} copy(bf16[16,8,24,2048]{3,2,1,0:T(8,128)(2,1)} %bitcast.25) | data formatting | bytes 25165824
  21.9 0.0 copy-done.1
  21.9 0.4 copy.6
  22.4 0.0 copy-start
  22.4 7.7 %mul.129 = bf16[128,24,16,128]{3,2,1,0:T(8,128)(2,1)S(1)} broadcast(bf16[128,24,16]{2,1,0:T(8,128)(2,1)S(1)} %copy.6), dimensions={0,1,2} | broadcast | bytes 12681216 | tf_op jit(solution)/shard_map/mul | solution.py:54
  30.1 0.0 copy-done
  30.1 35.1 %fusion = bf16[49152,128]{0,1:T(8,128)(2,1)} fusion(bf16[128,49152]{1,0:T(8,128)(2,1)S(1)} %bitcast.23, bf16[16,8,384,128]{3,2,1,0:T(8,128)(2,1)S(1)} %bitcast.24), kind=kLoop, calls=%fused_computation.1 | loop fusion | flops 6291456 | bytes 37748736 | tf_op jit(solution)/shard_map/ma,lax->mlx/dot_general | solution.py:90
  65.2 16.6 %copy.7 = bf16[49152,128]{1,0:T(8,128)(2,1)} copy(bf16[49152,128]{0,1:T(8,128)(2,1)} %fusion) | data formatting | bytes 25165824 | tf_op jit(solution)/shard_map/ma,lax->mlx/dot_general | solution.py:90
  81.9 0.0 copy-start.2
  81.9 9.1 %convolution_bitcast_fusion = f32[6,1,24,2048]{3,0,2,1:T(8,128)} fusion(bf16[24,2048,128]{2,1,0:T(8,128)(2,1)} %bitcast.22, bf16[6,128]{1,0:T(8,128)(2,1)S(1)} %stack.10), kind=kOutput, calls=%fused_computation.2 | convolution fusion | flops 75497472 | bytes 13764096 | tf_op jit(solution)/shard_map/ma,lax->mlx/dot_general | solution.py:90
  91.0 0.0 all-reduce.3.cloned.1.call-update
  91.0 0.0 copy-done.2
  91.1 94.9 %all-reduce.3.cloned.1.call-done = f32[6,1,24,2048]{3,0,2,1:T(8,128)} async-done(((f32[6,1,24,2048]{3,0,2,1:T(8,128)}), f32[6,1,24,2048]{3,0,2,1:T(8,128)}) %all-reduce.3.cloned.1.call-update) | async-done | bytes 1179664 | tf_op jit(solution)/shard_map/psum | solution.py:96
  185.9 3.4 %slice_divide_fusion = (f32[1,1,24,2048]{3,0,2,1:T(1,128)S(1)}, f32[1,1,24,2048]{3,0,2,1:T(1,128)S(1)}) fusion(f32[6,1,24,2048]{3,0,2,1:T(8,128)} %all-reduce.3.cloned.1.call-done), kind=kLoop, calls=%fused_computation.5 | loop fusion | flops 98304 | bytes 983040 | tf_op jit(solution)/shard_map/div | solution.py:62
  189.3 0.2 fusion.3
  189.6 1.9 collective-permute-start.1
  191.5 3.6 %collective-permute-start = (f32[2,1,1,258]{3,0,2,1:T(2,128)S(1)}, f32[2,1,1,258]{3,0,2,1:T(2,128)S(1)}, u32[]{:S(2)}, u32[]{:S(2)}) collective-permute-start(f32[2,1,1,258]{3,0,2,1:T(2,128)S(1)} %get-tuple-element.14), channel_id=1, source_target_pairs={{2,0},{4,2},{6,4},{8,6},{10,8},{12,10},{14,12},{16,14},{18,16},{20... | collective-permute-start | bytes 6200 | tf_op jit(solution)/shard_map/ppermute | solution.py:23
  195.1 1.7 multiply_subtract_fusion.2
  196.9 0.1 maximum_multiply_fusion
  197.0 0.6 copy.9
  197.6 0.0 collective-permute-done.1
  197.6 0.0 collective-permute-done
  197.7 4.0 %collective-permute-start.3 = (f32[2,1,26,258]{3,0,2,1:T(2,128)S(1)}, f32[2,1,26,258]{3,0,2,1:T(2,128)S(1)}, u32[]{:S(2)}, u32[]{:S(2)}) collective-permute-start(f32[2,1,26,258]{3,0,2,1:T(2,128)S(1)} %pad_maximum_fusion), channel_id=1, source_target_pairs={{0,1},{2,3},{4,5},{6,7},{8,9},{10,11},{12,13},{14,15},{16,17},{18,... | collective-permute-start | bytes 161000 | tf_op jit(solution)/shard_map/ppermute | solution.py:21
  201.6 1.3 collective-permute-start.2
  202.9 0.3 fusion.6
  203.2 0.1 fusion.16
  203.3 0.6 copy.8
  203.9 0.0 collective-permute-done.3
  203.9 4.0 %collective-permute-done.2 = f32[2,1,26,258]{3,0,2,1:T(2,128)S(1)} collective-permute-done((f32[2,1,26,258]{3,0,2,1:T(2,128)S(1)}, f32[2,1,26,258]{3,0,2,1:T(2,128)S(1)}, u32[]{:S(2)}, u32[]{:S(2)}) %collective-permute-start.2) | collective-permute-done | bytes 53696 | tf_op jit(solution)/shard_map/ppermute | solution.py:23
  208.0 0.2 fusion.5
  208.1 0.2 stack.13
  208.4 0.7 copy.10
  (10 shorter events, 0.2 us)
Async XLA Ops:
  7.2 178.8 %all-reduce.3.cloned.1.call-start = ((), (), s32[]{:S(2)}) async-start(), calls=%async_computation | async-start | bytes 3145728 | tf_op jit(solution)/shard_map/psum | solution.py:96
  7.3 14.6 %copy-start.1 = (s32[1,128,24,16]{1,3,2,0:T(8,128)S(1)}, s32[1,128,24,16]{1,3,2,0:T(8,128)}, u32[]{:S(2)}) copy-start(s32[1,128,24,16]{1,3,2,0:T(8,128)} %param.4) | copy-start | bytes 589828
  22.4 7.7 %copy-start = (bf16[16,8,24,2048]{3,1,2,0:T(8,128)(2,1)S(1)}, bf16[16,8,24,2048]{3,1,2,0:T(8,128)(2,1)}, u32[]{:S(2)}) copy-start(bf16[16,8,24,2048]{3,1,2,0:T(8,128)(2,1)} %copy.11) | copy-start | bytes 37748740
  81.9 9.2 %copy-start.2 = (s32[1,24,256]{2,1,0:T(8,128)S(1)}, s32[1,24,256]{2,1,0:T(8,128)}, u32[]{:S(2)}) copy-start(s32[1,24,256]{2,1,0:T(8,128)} %param.5) | copy-start | bytes 73732
  189.6 8.1 %collective-permute-start.1 = (f32[2,1,1,258]{3,0,2,1:T(2,128)S(1)}, f32[2,1,1,258]{3,0,2,1:T(2,128)S(1)}, u32[]{:S(2)}, u32[]{:S(2)}) collective-permute-start(f32[2,1,1,258]{3,0,2,1:T(2,128)S(1)} %get-tuple-element.15), channel_id=1, source_target_pairs={{0,2},{2,4},{4,6},{6,8},{8,10},{10,12},{12,14},{14,16},{16,18},{18... | collective-permute-start | bytes 6200 | tf_op jit(solution)/shard_map/ppermute | solution.py:21
  191.5 6.1 %collective-permute-start = (f32[2,1,1,258]{3,0,2,1:T(2,128)S(1)}, f32[2,1,1,258]{3,0,2,1:T(2,128)S(1)}, u32[]{:S(2)}, u32[]{:S(2)}) collective-permute-start(f32[2,1,1,258]{3,0,2,1:T(2,128)S(1)} %get-tuple-element.14), channel_id=1, source_target_pairs={{2,0},{4,2},{6,4},{8,6},{10,8},{12,10},{14,12},{16,14},{18,16},{20... | collective-permute-start | bytes 6200 | tf_op jit(solution)/shard_map/ppermute | solution.py:23
  197.7 6.3 %collective-permute-start.3 = (f32[2,1,26,258]{3,0,2,1:T(2,128)S(1)}, f32[2,1,26,258]{3,0,2,1:T(2,128)S(1)}, u32[]{:S(2)}, u32[]{:S(2)}) collective-permute-start(f32[2,1,26,258]{3,0,2,1:T(2,128)S(1)} %pad_maximum_fusion), channel_id=1, source_target_pairs={{0,1},{2,3},{4,5},{6,7},{8,9},{10,11},{12,13},{14,15},{16,17},{18,... | collective-permute-start | bytes 161000 | tf_op jit(solution)/shard_map/ppermute | solution.py:21
  201.6 6.3 %collective-permute-start.2 = (f32[2,1,26,258]{3,0,2,1:T(2,128)S(1)}, f32[2,1,26,258]{3,0,2,1:T(2,128)S(1)}, u32[]{:S(2)}, u32[]{:S(2)}) collective-permute-start(f32[2,1,26,258]{3,0,2,1:T(2,128)S(1)} %pad_maximum_fusion), channel_id=1, source_target_pairs={{1,0},{3,2},{5,4},{7,6},{9,8},{11,10},{13,12},{15,14},{17,16},{19,... | collective-permute-start | bytes 161000 | tf_op jit(solution)/shard_map/ppermute | solution.py:23
Sparse Core Ops, SparseCore 0:
  91.1 94.7 all-reduce.2
where the time goes:
time: 219 us; the launch traced here: 216 us
  waiting for transfers between devices  98.9 us (45%)
  local copies, waits for them, and re-layouts  41.6 us (19%)
  other arithmetic  41.2 us (19%)
  between operations  14.2 us (6%)
  starting transfers between devices  10.9 us (5%)
  matrix products  9.1 us (4%)
    psum x1, waiting for transfers between devices, on_device(): summed_all = lax.psum(partial_value, 'angle')  94.9 us
    dot_general x1, other arithmetic, on_device(): jnp.einsum('ma,lax->mlx', angle_weights, intensity, preferred_element_typ...  35.1 us
    dot_general x1, local copies, waits for them, and re-layouts, on_device(): jnp.einsum('ma,lax->mlx', angle_weights, intensity, preferred_element_typ...  16.6 us
    unnamed x10, local copies, waits for them, and re-layouts  16.6 us
    dot_general x1, matrix products, on_device(): jnp.einsum('ma,lax->mlx', angle_weights, intensity, preferred_element_typ...  9.1 us
    mul x2, local copies, waits for them, and re-layouts, intensity_of(): frames.reshape(layers_here, angles_here, rows_here, blocks, columns // bl...  8.12 us
    ppermute x2, starting transfers between devices, padded_2(): lax.ppermute(tail, axis, [(i, (i + 1) % count) for i in range(ends)])  5.9 us
    ppermute x2, starting transfers between devices, padded_2(): lax.ppermute(head, axis, [((i + 1) % count, i) for i in range(ends)])  4.93 us
  transfers between devices with their start and end apart: 5, of which 2 were waited for; matrix products, arithmetic and copies ran while one was open for 2% of the time, Pallas kernels for 0%

commit v1 on v0

v1 whole, which is shorter than its diff:
```python
import functools

import jax
import jax.numpy as jnp
from jax import lax
from jax.experimental import pallas as pl
from jax.experimental.pallas import tpu as pltpu
from jax.sharding import PartitionSpec as P

NPHI = 32
NCHI = 32
MOMENTS = 6
ROWS = 24
ANGLES_HERE = 128
LANES = 128
HALF = ANGLES_HERE // 2
DEPTH = HALF * 16
LAYER_PITCH = 2.0
MESH = pl.DeviceIdType.MESH


def fill_tables(me, spread_ref, weight_ref):
    lane = lax.broadcasted_iota(jnp.int32, (ANGLES_HERE, DEPTH), 1)
    source = lax.broadcasted_iota(jnp.int32, (ANGLES_HERE, DEPTH), 0)
    pair = lane >> 4
    for parity in range(2):
        hit = source == 2 * pair + parity
        spread_ref[parity * ANGLES_HERE : (parity + 1) * ANGLES_HERE, :] = jnp.where(
            hit, 1.0, 0.0
        ).astype(jnp.bfloat16)
    lane = lax.broadcasted_iota(jnp.int32, (16, DEPTH), 1)
    row = lax.broadcasted_iota(jnp.int32, (16, DEPTH), 0)
    inner = lane & 15
    keep = inner == row
    for kind in range(3):
        if kind == 0:
            parity = 0
        elif kind == 2:
            parity = 1
        else:
            parity = inner >> 3
        angle = me * ANGLES_HERE + 2 * (lane >> 4) + parity
        phi = ((angle >> 5).astype(jnp.float32) - 0.5 * (NPHI - 1)) / (0.5 * NPHI)
        chi = ((angle & 31).astype(jnp.float32) - 0.5 * (NCHI - 1)) / (0.5 * NCHI)
        rows = (jnp.ones_like(phi), phi, chi, phi * phi, chi * chi, phi * chi)
        for m in range(MOMENTS):
            weight_ref[kind, m] = jnp.where(keep, rows[m], 0.0).astype(jnp.bfloat16)


def fill_factors(exp_ref, factor_ref):
    blank = jnp.zeros((8, ANGLES_HERE), jnp.float32)

    def one(k, carry):
        code = exp_ref[pl.ds(k, ROWS, stride=16), :]
        factor = jnp.exp2(code.astype(jnp.float32))
        low, mid, high = factor[0:8], factor[8:16], factor[16:24]
        even = jnp.concatenate([low, mid, high, blank, blank, blank], axis=0)
        odd = jnp.concatenate([blank, blank, blank, low, mid, high], axis=0)
        both = jnp.concatenate([even, odd], axis=1)
        factor_ref[k] = both.astype(jnp.bfloat16)
        return carry

    lax.fori_loop(0, 16, one, 0)


def partial_moments(dest, slot, buf, factor_ref, spread_ref, weight_ref, out_ref):
    for side in range(2):
        grown = jnp.dot(
            factor_ref[2 * dest + side], spread_ref[...], preferred_element_type=jnp.float32
        ).astype(jnp.bfloat16)
        sums = []
        for kind in range(3):
            left = (
                weight_ref[kind] * grown[kind * 16 : kind * 16 + 16][None]
            ).reshape(MOMENTS * 16, DEPTH)
            right = buf[
                slot, :, kind * 16 : kind * 16 + 16, side * LANES : (side + 1) * LANES
            ].reshape(DEPTH, LANES)
            sums.append(
                jnp.dot(left, right, preferred_element_type=jnp.float32).reshape(
                    MOMENTS, 16, LANES
                )
            )
        first, second, third = sums
        here = slice(side * LANES, (side + 1) * LANES)
        out_ref[slot, :, 0:8, here] = first[:, 0:8] + second[:, 8:16]
        out_ref[slot, :, 8:16, here] = first[:, 8:16] + third[:, 0:8]
        out_ref[slot, :, 16:24, here] = second[:, 0:8] + third[:, 8:16]


def kernel(
    count, tiles, frames, exponents, valid,
    orient_out, spread_out, nye_out,
    buf, exp_ref, mask_ref, factor_ref, spread_ref, weight_ref,
    send, recv, orient, left_halo, right_halo, up_halo, down_halo, layer_halo,
    in_sem, small_sem, send_sem, recv_sem, halo_send, halo_recv,
):
    me = lax.axis_index("angle")
    tile = lax.axis_index("tile")
    layer = lax.axis_index("layer")
    cols = 2 * LANES

    exp_copy = pltpu.make_async_copy(exponents, exp_ref, small_sem.at[0])
    exp_copy.start()

    def chunk(step):
        dest = lax.rem(me + 1 + step, count)
        begin = pl.multiple_of(dest * cols, cols)
        return pltpu.make_async_copy(
            frames.at[:, :, pl.ds(begin, cols)], buf.at[step], in_sem.at[step]
        )

    for step in range(count):
        chunk(step).start()
    mask_copy = pltpu.make_async_copy(valid, mask_ref, small_sem.at[1])
    mask_copy.start()

    barrier = pltpu.get_barrier_semaphore()
    for step in range(count - 1):
        pl.semaphore_signal(
            barrier, inc=1, device_id={"angle": lax.rem(me + 1 + step, count)},
            device_id_type=MESH,
        )
    pl.semaphore_signal(barrier, inc=1, device_id={"layer": 1 - layer}, device_id_type=MESH)

    @pl.when(tile > 0)
    def _():
        pl.semaphore_signal(barrier, inc=1, device_id={"tile": tile - 1}, device_id_type=MESH)

    @pl.when(tile < tiles - 1)
    def _():
        pl.semaphore_signal(barrier, inc=1, device_id={"tile": tile + 1}, device_id_type=MESH)

    fill_tables(me, spread_ref, weight_ref)
    exp_copy.wait()
    fill_factors(exp_ref, factor_ref)

    near = (tile > 0).astype(jnp.int32) + (tile < tiles - 1).astype(jnp.int32)
    pl.semaphore_wait(barrier, count + near)

    def remote(step):
        return pltpu.make_async_remote_copy(
            src_ref=send.at[step],
            dst_ref=recv.at[step],
            send_sem=send_sem.at[step],
            recv_sem=recv_sem.at[step],
            device_id={"angle": lax.rem(me + 1 + step, count)},
            device_id_type=MESH,
        )

    def one(step, carry):
        chunk(step).wait()
        partial_moments(
            lax.rem(me + 1 + step, count), step, buf, factor_ref, spread_ref, weight_ref, send
        )

        @pl.when(step < count - 1)
        def _():
            remote(step).start()

        return carry

    lax.fori_loop(0, count, one, 0)

    total = send[count - 1]
    for step in range(count - 1):
        remote(step).wait_recv()
        total = total + recv[step]

    field = [total[1] / total[0], total[2] / total[0]]
    orient[0] = field[0]
    orient[1] = field[1]

    def halo(index, src, dst, where):
        return pltpu.make_async_remote_copy(
            src_ref=src, dst_ref=dst, send_sem=halo_send.at[index],
            recv_sem=halo_recv.at[index], device_id=where, device_id_type=MESH,
        )

    to_layer = halo(0, orient, layer_halo, {"layer": 1 - layer})
    to_next_tile = halo(1, orient.at[:, 16:24, :], up_halo, {"tile": tile + 1})
    to_last_tile = halo(2, orient.at[:, 0:8, :], down_halo, {"tile": tile - 1})
    to_next_angle = halo(3, orient.at[:, :, LANES:cols], left_halo, {"angle": me + 1})
    to_last_angle = halo(4, orient.at[:, :, 0:LANES], right_halo, {"angle": me - 1})
    has_next_tile = tile < tiles - 1
    has_last_tile = tile > 0
    has_next_angle = me < count - 1
    has_last_angle = me > 0
    to_layer.start()
    pl.when(has_next_tile)(lambda: to_next_tile.start())
    pl.when(has_last_tile)(lambda: to_last_tile.start())
    pl.when(has_next_angle)(lambda: to_next_angle.start())
    pl.when(has_last_angle)(lambda: to_last_angle.start())

    @pl.when(jnp.logical_not(has_last_tile))
    def _():
        up_halo[...] = jnp.zeros_like(up_halo)

    @pl.when(jnp.logical_not(has_next_tile))
    def _():
        down_halo[...] = jnp.zeros_like(down_halo)

    @pl.when(jnp.logical_not(has_last_angle))
    def _():
        left_halo[...] = jnp.zeros_like(left_halo)

    @pl.when(jnp.logical_not(has_next_angle))
    def _():
        right_halo[...] = jnp.zeros_like(right_halo)

    mask_copy.wait()
    mask = mask_ref[...].astype(jnp.float32)
    orient_out[0] = field[0] * mask
    orient_out[1] = field[1] * mask
    spread_out[0] = (total[3] / total[0] - field[0] * field[0]) * mask
    spread_out[1] = (total[4] / total[0] - field[1] * field[1]) * mask
    spread_out[2] = (total[5] / total[0] - field[0] * field[1]) * mask

    pl.when(has_last_tile)(lambda: to_next_tile.wait_recv())
    pl.when(has_next_tile)(lambda: to_last_tile.wait_recv())
    pl.when(has_last_angle)(lambda: to_next_angle.wait_recv())
    pl.when(has_next_angle)(lambda: to_last_angle.wait_recv())

    lane = lax.broadcasted_iota(jnp.int32, (ROWS, cols), 1)
    row = lax.broadcasted_iota(jnp.int32, (ROWS, cols), 0)
    along_x, along_y = [], []
    for f in range(2):
        after = jnp.where(
            lane == cols - 1, right_halo[f, :, 0:1], pltpu.roll(field[f], cols - 1, 1)
        )
        before = jnp.where(
            lane == 0, left_halo[f, :, LANES - 1 : LANES], pltpu.roll(field[f], 1, 1)
        )
        along_x.append(0.5 * (after - before))
        after = jnp.where(row == ROWS - 1, down_halo[f, 0:1, :], pltpu.roll(field[f], ROWS - 1, 0))
        before = jnp.where(row == 0, up_halo[f, 7:8, :], pltpu.roll(field[f], 1, 0))
        along_y.append(0.5 * (after - before))
    nye_out[0] = -along_y[1] * mask
    nye_out[1] = -along_x[0] * mask
    nye_out[2] = -(along_x[0] + along_y[1]) * mask
    nye_out[3] = along_x[1] * mask
    nye_out[4] = along_y[0] * mask
    to_layer.wait_recv()
    slope = (0.5 / LAYER_PITCH) * (1 - 2 * layer).astype(jnp.float32) * mask
    nye_out[5] = layer_halo[0] * slope
    nye_out[6] = layer_halo[1] * slope

    for step in range(count - 1):
        remote(step).wait_send()
    to_layer.wait_send()
    pl.when(has_next_tile)(lambda: to_next_tile.wait_send())
    pl.when(has_last_tile)(lambda: to_last_tile.wait_send())
    pl.when(has_next_angle)(lambda: to_next_angle.wait_send())
    pl.when(has_last_angle)(lambda: to_last_angle.wait_send())


def on_device(count, tiles, frames, exponents, valid_mask):
    columns = frames.shape[3]
    cols = columns // count
    stack = frames.reshape(HALF, 2 * ROWS, columns)
    codes = exponents[0].transpose(1, 2, 0).reshape(ROWS * 16, ANGLES_HERE)
    f32 = jnp.float32
    bf16 = jnp.bfloat16
    anywhere = pl.BlockSpec(memory_space=pl.ANY)
    vmem = pl.BlockSpec(memory_space=pltpu.VMEM)
    out = pl.pallas_call(
        functools.partial(kernel, count, tiles),
        out_shape=[
            jax.ShapeDtypeStruct((2, ROWS, cols), f32),
            jax.ShapeDtypeStruct((3, ROWS, cols), f32),
            jax.ShapeDtypeStruct((7, ROWS, cols), f32),
        ],
        in_specs=[anywhere] * 3,
        out_specs=[vmem] * 3,
        scratch_shapes=[
            pltpu.VMEM((count, HALF, 2 * ROWS, cols), bf16),
            pltpu.VMEM((ROWS * 16, ANGLES_HERE), jnp.int32),
            pltpu.VMEM((ROWS, cols), jnp.int32),
            pltpu.VMEM((16, 48, 2 * ANGLES_HERE), bf16),
            pltpu.VMEM((2 * ANGLES_HERE, DEPTH), bf16),
            pltpu.VMEM((3, MOMENTS, 16, DEPTH), bf16),
            pltpu.VMEM((count, MOMENTS, ROWS, cols), f32),
            pltpu.VMEM((count - 1, MOMENTS, ROWS, cols), f32),
            pltpu.VMEM((2, ROWS, cols), f32),
            pltpu.VMEM((2, ROWS, LANES), f32),
            pltpu.VMEM((2, ROWS, LANES), f32),
            pltpu.VMEM((2, 8, cols), f32),
            pltpu.VMEM((2, 8, cols), f32),
            pltpu.VMEM((2, ROWS, cols), f32),
            pltpu.SemaphoreType.DMA((count,)),
            pltpu.SemaphoreType.DMA((2,)),
            pltpu.SemaphoreType.DMA((count - 1,)),
            pltpu.SemaphoreType.DMA((count - 1,)),
            pltpu.SemaphoreType.DMA((5,)),
            pltpu.SemaphoreType.DMA((5,)),
        ],
        compiler_params=pltpu.CompilerParams(
            collective_id=0, has_side_effects=True, vmem_limit_bytes=60 * 1024 * 1024
        ),
    )(stack, codes, valid_mask[0])
    return tuple(part[:, None] for part in out)


def solution(mesh):
    in_specs = (
        P("layer", "angle", "tile", None),
        P("layer", "angle", "tile", None),
        P("layer", "tile", "angle"),
    )
    out_specs = (
        P(None, "layer", "tile", "angle"),
        P(None, "layer", "tile", "angle"),
        P(None, "layer", "tile", "angle"),
    )
    return jax.shard_map(
        functools.partial(on_device, mesh.shape["angle"], mesh.shape["tile"]),
        mesh=mesh, in_specs=in_specs, out_specs=out_specs, check_vma=False,
    )
```

time: 219 us -> 37.8 us (0.17); the launches traced: 216 us -> 37.4 us
  waiting for transfers between devices: 98.9 us -> 0 us
  other arithmetic: 41.2 us -> 0 us
  local copies, waits for them, and re-layouts: 41.6 us -> 4.54 us
  Pallas kernels: 0 us -> 32.2 us
  between operations: 14.2 us -> 0.64 us
  starting transfers between devices: 10.9 us -> 0 us
  matrix products: 9.1 us -> 0 us
    psum x1 -> x0, waiting for transfers between devices: 94.9 us -> none  [on_device(): summed_all = lax.psum(partial_value, 'angle')]
    dot_general x1 -> x0, other arithmetic: 35.1 us -> none  [on_device(): jnp.einsum('ma,lax->mlx', angle_weights, intensity, preferred_element_typ...]
    pallas_call x0 -> x1, Pallas kernels: none -> 32.2 us  [on_device(): pl.pallas_call(functools.partial(kernel, count, tiles), out_shape=[jax.Sh...]
    dot_general x1 -> x0, local copies, waits for them, and re-layouts: 16.6 us -> none  [on_device(): jnp.einsum('ma,lax->mlx', angle_weights, intensity, preferred_element_typ...]
    unnamed x10 -> x3, local copies, waits for them, and re-layouts: 16.6 us -> 4.54 us
    ppermute x4 -> x0, starting transfers between devices: 10.8 us -> none  [the longest x2 5.9 us: padded_2(): lax.ppermute(tail, axis, [(i, (i + 1) % count) for i in range(ends)])]
    dot_general x1 -> x0, matrix products: 9.1 us -> none  [on_device(): jnp.einsum('ma,lax->mlx', angle_weights, intensity, preferred_element_typ...]
    mul x2 -> x0, local copies, waits for them, and re-layouts: 8.12 us -> none  [intensity_of(): frames.reshape(layers_here, angles_here, rows_here, blocks, columns // bl...]
  transfers between devices with their start and end apart: 5 -> 0, of which waited for: 2 -> 0; matrix products, arithmetic and copies ran while one was open for 2% -> 0% of each run, Pallas kernels for 0% -> 0%
where the time goes in v1:
time: 37.8 us; the launch traced here: 37.4 us
  Pallas kernels  32.2 us (85%)
  local copies, waits for them, and re-layouts  4.54 us (12%)
  between operations  0.64 us (2%)
    pallas_call x1, Pallas kernels, on_device(): pl.pallas_call(functools.partial(kernel, count, tiles), out_shape=[jax.Sh...  32.2 us
    unnamed x3, local copies, waits for them, and re-layouts  4.54 us

profile of v1, /device:TPU:100, one launch (start us, length us, event | category | flops | bytes accessed | tf_op | source)
XLA Modules:
  0.0 37.4 jit_solution(7196273630870780291)
XLA Ops:
  0.6 32.2 %shard_map.58 = (f32[2,24,256]{2,1,0:T(8,128)}, f32[3,24,256]{2,1,0:T(8,128)}, f32[7,24,256]{2,1,0:T(8,128)}) custom-call(bf16[64,48,2048]{2,1,0:T(8,128)(2,1)} %bitcast.16, s32[384,128]{1,0:T(8,128)} %bitcast.17, s32[24,256]{1,0:T(8,128)} %bitcast.21), custom_call_target="tpu_custom_call" | custom-call | tf_op jit(solution)/shard_map/pallas_call | solution.py:266
  32.9 1.4 %copy.12 = f32[2,1,24,256]{3,2,1,0:T(8,128)} copy(f32[2,1,24,256]{3,2,1,0:T(8,128)} %bitcast.20) | data formatting | bytes 98304
  34.3 1.5 %copy.13 = f32[3,1,24,256]{3,2,1,0:T(8,128)} copy(f32[3,1,24,256]{3,2,1,0:T(8,128)} %bitcast.19) | data formatting | bytes 147456
  35.8 1.6 %copy.14 = f32[7,1,24,256]{3,2,1,0:T(8,128)} copy(f32[7,1,24,256]{3,2,1,0:T(8,128)} %bitcast.18) | data formatting | bytes 344064

commit v2 on v1

v2 whole, which is shorter than its diff:
```python
import functools

import jax
import jax.numpy as jnp
from jax import lax
from jax.experimental import pallas as pl
from jax.experimental.pallas import tpu as pltpu
from jax.sharding import PartitionSpec as P

NPHI = 32
NCHI = 32
MOMENTS = 6
ROWS = 24
ANGLES_HERE = 128
LANES = 128
HALF = ANGLES_HERE // 2
DEPTH = HALF * 16
LAYER_PITCH = 2.0
AHEAD = 3
ORDER = (0, 2, 1)
MESH = pl.DeviceIdType.MESH


def fill_tables(me, spread_ref, weight_ref):
    lane = lax.broadcasted_iota(jnp.int32, (ANGLES_HERE, DEPTH), 1)
    source = lax.broadcasted_iota(jnp.int32, (ANGLES_HERE, DEPTH), 0)
    pair = lane >> 4
    for parity in range(2):
        hit = source == 2 * pair + parity
        spread_ref[parity * ANGLES_HERE : (parity + 1) * ANGLES_HERE, :] = jnp.where(
            hit, 1.0, 0.0
        ).astype(jnp.bfloat16)
    lane = lax.broadcasted_iota(jnp.int32, (16, DEPTH), 1)
    row = lax.broadcasted_iota(jnp.int32, (16, DEPTH), 0)
    inner = lane & 15
    keep = inner == row
    for kind in range(3):
        if kind == 0:
            parity = 0
        elif kind == 2:
            parity = 1
        else:
            parity = inner >> 3
        angle = me * ANGLES_HERE + 2 * (lane >> 4) + parity
        phi = ((angle >> 5).astype(jnp.float32) - 0.5 * (NPHI - 1)) / (0.5 * NPHI)
        chi = ((angle & 31).astype(jnp.float32) - 0.5 * (NCHI - 1)) / (0.5 * NCHI)
        rows = (jnp.ones_like(phi), phi, chi, phi * phi, chi * chi, phi * chi)
        for m in range(MOMENTS):
            weight_ref[kind, m] = jnp.where(keep, rows[m], 0.0).astype(jnp.bfloat16)


def fill_factors(exp_ref, factor_ref):
    blank = jnp.zeros((8, ANGLES_HERE), jnp.float32)

    def one(k, carry):
        code = exp_ref[pl.ds(k, ROWS, stride=16), :]
        factor = jnp.exp2(code.astype(jnp.float32))
        low, mid, high = factor[0:8], factor[8:16], factor[16:24]
        even = jnp.concatenate([low, mid, high, blank, blank, blank], axis=0)
        odd = jnp.concatenate([blank, blank, blank, low, mid, high], axis=0)
        both = jnp.concatenate([even, odd], axis=1)
        factor_ref[k] = both.astype(jnp.bfloat16)
        return carry

    lax.fori_loop(0, 16, one, 0)


def grow(role, dest, factor_ref, spread_ref, grown_ref):
    both = factor_ref[pl.ds(2 * dest, 2)].reshape(96, 2 * ANGLES_HERE)
    grown_ref[lax.rem(role, 2)] = jnp.dot(
        both, spread_ref[...], preferred_element_type=jnp.float32
    ).astype(jnp.bfloat16)


def partial_moments(role, buf, grown_ref, weight_ref, part):
    slot = lax.rem(role, 2)
    for side in range(2):
        sums = []
        for kind in range(3):
            begin = side * 48 + kind * 16
            left = (weight_ref[kind] * grown_ref[slot, begin : begin + 16][None]).reshape(
                MOMENTS * 16, DEPTH
            )
            right = buf[
                role, :, kind * 16 : kind * 16 + 16, side * LANES : (side + 1) * LANES
            ].reshape(DEPTH, LANES)
            sums.append(
                jnp.dot(left, right, preferred_element_type=jnp.float32).reshape(
                    MOMENTS, 16, LANES
                )
            )
        first, second, third = sums
        here = slice(side * LANES, (side + 1) * LANES)
        part[role, :, 0:8, here] = first[:, 0:8] + second[:, 8:16]
        part[role, :, 8:16, here] = first[:, 8:16] + third[:, 0:8]
        part[role, :, 16:24, here] = second[:, 0:8] + third[:, 8:16]


def kernel(
    sizes, frames, exponents, valid, out,
    buf, exp_ref, mask_ref, factor_ref, spread_ref, weight_ref, grown_ref,
    part, early, halves, late, last, orient,
    left_halo, right_halo, up_halo, down_halo, layer_halo,
    in_sem, small_sem, early_send, early_recv, half_send, half_recv,
    late_send, late_recv, last_send, last_recv, halo_send, halo_recv,
):
    count, tiles = sizes
    ring = count // 2
    me = lax.axis_index("angle")
    tile = lax.axis_index("tile")
    layer = lax.axis_index("layer")
    cols = 2 * LANES
    px, py = me // ring, lax.rem(me, ring)
    other = (1 - px) * ring + py
    above = px * ring + lax.rem(py + 1, ring)
    below = px * ring + lax.rem(py + ring - 1, ring)
    has_next_tile = tile < tiles - 1
    has_last_tile = tile > 0
    has_next_angle = me < count - 1
    has_last_angle = me > 0
    far_next = me == ring - 1
    far_last = me == ring

    def owner(role):
        swap = jnp.logical_or(role < 3, role == 6)
        shift = jnp.where(role >= 6, 0, 2)
        turn = lax.rem(role, 3)
        shift = jnp.where(role < 6, jnp.where(turn == 0, 2, jnp.where(turn == 1, 1, ring - 1)), 0)
        return jnp.where(swap, 1 - px, px) * ring + lax.rem(py + shift, ring)

    def chunk(role):
        begin = pl.multiple_of(owner(role) * cols, cols)
        return pltpu.make_async_copy(
            frames.at[:, :, pl.ds(begin, cols)], buf.at[role], in_sem.at[role]
        )

    exp_copy = pltpu.make_async_copy(exponents, exp_ref, small_sem.at[0])
    mask_copy = pltpu.make_async_copy(valid, mask_ref, small_sem.at[1])
    exp_copy.start()
    for role in range(AHEAD):
        chunk(jnp.int32(role)).start()

    barrier = pltpu.get_barrier_semaphore()

    def greet(where):
        pl.semaphore_signal(barrier, inc=1, device_id=where, device_id_type=MESH)

    greet({"angle": other})
    greet({"angle": above})
    greet({"angle": below})
    greet({"layer": 1 - layer})
    pl.when(has_last_tile)(lambda: greet({"tile": tile - 1}))
    pl.when(has_next_tile)(lambda: greet({"tile": tile + 1}))
    pl.when(far_next)(lambda: greet({"angle": me + 1}))
    pl.when(far_last)(lambda: greet({"angle": me - 1}))
    partners = 4
    for present in (has_last_tile, has_next_tile, far_next, far_last):
        partners = partners + present.astype(jnp.int32)

    fill_tables(me, spread_ref, weight_ref)
    exp_copy.wait()
    mask_copy.start()
    fill_factors(exp_ref, factor_ref)
    grow(jnp.int32(0), owner(jnp.int32(0)), factor_ref, spread_ref, grown_ref)

    def remote(src, dst, send, recv, where):
        return pltpu.make_async_remote_copy(
            src_ref=src, dst_ref=dst, send_sem=send, recv_sem=recv, device_id=where,
            device_id_type=MESH,
        )

    def rows(g):
        return pl.ds(8 * g, 8)

    def early_copy(role, g):
        to = jnp.where(role == 0, other, jnp.where(role == 1, above, below))
        return remote(
            part.at[role, :, rows(g), :], early.at[role, :, rows(g), :],
            early_send.at[role, g], early_recv.at[role, g], {"angle": to},
        )

    def half_copy(side, g):
        which = pl.ds(3 * side, 3)
        return remote(
            part.at[3, which, rows(g), :], halves.at[side, :, rows(g), :],
            half_send.at[side, g], half_recv.at[side, g],
            {"angle": below if side else above},
        )

    def late_copy(side, g):
        return remote(
            part.at[4 + side, :, rows(g), :], late.at[side, :, rows(g), :],
            late_send.at[side, g], late_recv.at[side, g],
            {"angle": below if side else above},
        )

    def last_copy(g):
        return remote(
            part.at[6, :, rows(g), :], last.at[:, rows(g), :], last_send.at[g], last_recv.at[g],
            {"angle": other},
        )

    def one(role, carry):
        chunk(role).wait()

        @pl.when(role + AHEAD < count)
        def _():
            chunk(role + AHEAD).start()

        following = jnp.minimum(role + 1, count - 1)
        grow(role + 1, owner(following), factor_ref, spread_ref, grown_ref)
        partial_moments(role, buf, grown_ref, weight_ref, part)

        @pl.when(role == 0)
        def _():
            pl.semaphore_wait(barrier, partners)

        @pl.when(role < 3)
        def _():
            for g in ORDER:
                early_copy(role, g).start()

        @pl.when(role == 5)
        def _():
            for g in ORDER:
                early_copy(0, g).wait_recv()
                part[3, :, 8 * g : 8 * g + 8] += early[0, :, 8 * g : 8 * g + 8]
                half_copy(0, g).start()
                half_copy(1, g).start()

        return carry

    lax.fori_loop(0, count, one, 0)

    for g in ORDER:
        here = slice(8 * g, 8 * g + 8)
        early_copy(1, g).wait_recv()
        early_copy(2, g).wait_recv()
        part[6, :, here] += early[1, :, here] + early[2, :, here]
        last_copy(g).start()
    for g in ORDER:
        here = slice(8 * g, 8 * g + 8)
        half_copy(0, g).wait_recv()
        part[4, 0:3, here] += halves[0, :, here]
        late_copy(0, g).start()
        half_copy(1, g).wait_recv()
        part[5, 3:6, here] += halves[1, :, here]
        late_copy(1, g).start()

    @pl.when(jnp.logical_not(has_last_tile))
    def _():
        up_halo[...] = jnp.zeros_like(up_halo)

    @pl.when(jnp.logical_not(has_next_tile))
    def _():
        down_halo[...] = jnp.zeros_like(down_halo)

    @pl.when(jnp.logical_not(has_last_angle))
    def _():
        left_halo[...] = jnp.zeros_like(left_halo)

    @pl.when(jnp.logical_not(has_next_angle))
    def _():
        right_halo[...] = jnp.zeros_like(right_halo)

    def to_layer(g):
        return remote(
            orient.at[:, rows(g), :], layer_halo.at[:, rows(g), :],
            halo_send.at[0, g], halo_recv.at[0, g], {"layer": 1 - layer},
        )

    def to_next_angle(g):
        return remote(
            orient.at[:, rows(g), LANES:cols], left_halo.at[:, rows(g), :],
            halo_send.at[1, g], halo_recv.at[1, g], {"angle": me + 1},
        )

    def to_last_angle(g):
        return remote(
            orient.at[:, rows(g), 0:LANES], right_halo.at[:, rows(g), :],
            halo_send.at[2, g], halo_recv.at[2, g], {"angle": me - 1},
        )

    to_next_tile = remote(
        orient.at[:, rows(2), :], up_halo, halo_send.at[3, 0], halo_recv.at[3, 0],
        {"tile": tile + 1},
    )
    to_last_tile = remote(
        orient.at[:, rows(0), :], down_halo, halo_send.at[3, 1], halo_recv.at[3, 1],
        {"tile": tile - 1},
    )

    mask_copy.wait()
    for g in ORDER:
        here = slice(8 * g, 8 * g + 8)
        late_copy(0, g).wait_recv()
        late_copy(1, g).wait_recv()
        last_copy(g).wait_recv()
        total = part[7, :, here] + (late[0, :, here] + late[1, :, here]) + last[:, here]
        field = [total[1] / total[0], total[2] / total[0]]
        orient[0, here] = field[0]
        orient[1, here] = field[1]
        to_layer(g).start()
        pl.when(has_next_angle)(lambda: to_next_angle(g).start())
        pl.when(has_last_angle)(lambda: to_last_angle(g).start())
        if g == 0:
            pl.when(has_last_tile)(lambda: to_last_tile.start())
        if g == 2:
            pl.when(has_next_tile)(lambda: to_next_tile.start())
        mask = mask_ref[here].astype(jnp.float32)
        out[0, here] = field[0] * mask
        out[1, here] = field[1] * mask
        out[2, here] = (total[3] / total[0] - field[0] * field[0]) * mask
        out[3, here] = (total[4] / total[0] - field[1] * field[1]) * mask
        out[4, here] = (total[5] / total[0] - field[0] * field[1]) * mask

    pl.when(has_last_tile)(lambda: to_next_tile.wait_recv())
    pl.when(has_next_tile)(lambda: to_last_tile.wait_recv())
    for g in ORDER:
        pl.when(has_last_angle)(lambda: to_next_angle(g).wait_recv())
        pl.when(has_next_angle)(lambda: to_last_angle(g).wait_recv())

    mask = mask_ref[...].astype(jnp.float32)
    lane = lax.broadcasted_iota(jnp.int32, (ROWS, cols), 1)
    row = lax.broadcasted_iota(jnp.int32, (ROWS, cols), 0)
    along_x, along_y = [], []
    for f in range(2):
        field = orient[f]
        after = jnp.where(
            lane == cols - 1, right_halo[f, :, 0:1], pltpu.roll(field, cols - 1, 1)
        )
        before = jnp.where(lane == 0, left_halo[f, :, LANES - 1 : LANES], pltpu.roll(field, 1, 1))
        along_x.append(0.5 * (after - before))
        after = jnp.where(row == ROWS - 1, down_halo[f, 0:1, :], pltpu.roll(field, ROWS - 1, 0))
        before = jnp.where(row == 0, up_halo[f, 7:8, :], pltpu.roll(field, 1, 0))
        along_y.append(0.5 * (after - before))
    out[5] = -along_y[1] * mask
    out[6] = -along_x[0] * mask
    out[7] = -(along_x[0] + along_y[1]) * mask
    out[8] = along_x[1] * mask
    out[9] = along_y[0] * mask
    for g in ORDER:
        to_layer(g).wait_recv()
    slope = (0.5 / LAYER_PITCH) * (1 - 2 * layer).astype(jnp.float32) * mask
    out[10] = layer_halo[0] * slope
    out[11] = layer_halo[1] * slope

    for g in ORDER:
        for role in range(3):
            early_copy(role, g).wait_send()
        for side in range(2):
            half_copy(side, g).wait_send()
            late_copy(side, g).wait_send()
        last_copy(g).wait_send()
        to_layer(g).wait_send()
        pl.when(has_next_angle)(lambda: to_next_angle(g).wait_send())
        pl.when(has_last_angle)(lambda: to_last_angle(g).wait_send())
    pl.when(has_next_tile)(lambda: to_next_tile.wait_send())
    pl.when(has_last_tile)(lambda: to_last_tile.wait_send())


def write_out(maps, orient_out, spread_out, nye_out, sem):
    copies = [
        pltpu.make_async_copy(maps.at[0:2], orient_out, sem.at[0]),
        pltpu.make_async_copy(maps.at[2:5], spread_out, sem.at[1]),
        pltpu.make_async_copy(maps.at[5:12], nye_out, sem.at[2]),
    ]
    for copy in copies:
        copy.start()
    for copy in copies:
        copy.wait()


def on_device(count, tiles, frames, exponents, valid_mask):
    columns = frames.shape[3]
    cols = columns // count
    stack = frames.reshape(HALF, 2 * ROWS, columns)
    codes = exponents[0].transpose(1, 2, 0).reshape(ROWS * 16, ANGLES_HERE)
    f32 = jnp.float32
    bf16 = jnp.bfloat16
    dma = pltpu.SemaphoreType.DMA
    hbm = pl.BlockSpec(memory_space=pltpu.HBM)
    vmem = pl.BlockSpec(memory_space=pltpu.VMEM)
    block = (MOMENTS, ROWS, cols)
    maps = pl.pallas_call(
        functools.partial(kernel, (count, tiles)),
        out_shape=jax.ShapeDtypeStruct((12, ROWS, cols), f32),
        in_specs=[pl.BlockSpec(memory_space=pl.ANY)] * 3,
        out_specs=vmem,
        scratch_shapes=[
            pltpu.VMEM((count, HALF, 2 * ROWS, cols), bf16),
            pltpu.VMEM((ROWS * 16, ANGLES_HERE), jnp.int32),
            pltpu.VMEM((ROWS, cols), jnp.int32),
            pltpu.VMEM((16, 48, 2 * ANGLES_HERE), bf16),
            pltpu.VMEM((2 * ANGLES_HERE, DEPTH), bf16),
            pltpu.VMEM((3, MOMENTS, 16, DEPTH), bf16),
            pltpu.VMEM((2, 96, DEPTH), bf16),
            pltpu.VMEM((count,) + block, f32),
            pltpu.VMEM((3,) + block, f32),
            pltpu.VMEM((2, 3, ROWS, cols), f32),
            pltpu.VMEM((2,) + block, f32),
            pltpu.VMEM(block, f32),
            pltpu.VMEM((2, ROWS, cols), f32),
            pltpu.VMEM((2, ROWS, LANES), f32),
            pltpu.VMEM((2, ROWS, LANES), f32),
            pltpu.VMEM((2, 8, cols), f32),
            pltpu.VMEM((2, 8, cols), f32),
            pltpu.VMEM((2, ROWS, cols), f32),
            dma((count,)), dma((2,)), dma((3, 3)), dma((3, 3)), dma((2, 3)), dma((2, 3)),
            dma((2, 3)), dma((2, 3)), dma((3,)), dma((3,)), dma((4, 3)), dma((4, 3)),
        ],
        compiler_params=pltpu.CompilerParams(
            collective_id=0, has_side_effects=True, vmem_limit_bytes=52 * 1024 * 1024
        ),
    )(*(pltpu.with_memory_space_constraint(a, pltpu.HBM) for a in (stack, codes, valid_mask[0])))
    out = pl.pallas_call(
        write_out,
        out_shape=[jax.ShapeDtypeStruct((n, ROWS, cols), f32) for n in (2, 3, 7)],
        in_specs=[pl.BlockSpec(memory_space=pl.ANY)],
        out_specs=[hbm] * 3,
        scratch_shapes=[dma((3,))],
        compiler_params=pltpu.CompilerParams(vmem_limit_bytes=1024 * 1024),
    )(maps)
    return tuple(one[:, None] for one in out)


def solution(mesh):
    in_specs = (
        P("layer", "angle", "tile", None),
        P("layer", "angle", "tile", None),
        P("layer", "tile", "angle"),
    )
    out_specs = (
        P(None, "layer", "tile", "angle"),
        P(None, "layer", "tile", "angle"),
        P(None, "layer", "tile", "angle"),
    )
    return jax.shard_map(
        functools.partial(on_device, mesh.shape["angle"], mesh.shape["tile"]),
        mesh=mesh, in_specs=in_specs, out_specs=out_specs, check_vma=False,
    )
```

time: 37.8 us -> 24.7 us (0.65)
  Pallas kernels: 32.2 us -> 23.9 us
  local copies, waits for them, and re-layouts: 4.54 us -> 0 us
    pallas_call x1 -> x2, Pallas kernels: 32.2 us -> 23.9 us  [the longest x1 23.2 us: on_device(): pl.pallas_call(functools.partial(kernel, (count, tiles)), out_shape=jax.S...]
    unnamed x3 -> x0, local copies, waits for them, and re-layouts: 4.54 us -> none
where the time goes in v2:
time: 24.7 us; the launch traced here: 24.6 us
  Pallas kernels  23.9 us (97%)
  between operations  0.64 us (3%)
    pallas_call x1, Pallas kernels, on_device(): pl.pallas_call(functools.partial(kernel, (count, tiles)), out_shape=jax.S...  23.2 us
    pallas_call x1, Pallas kernels, on_device(): pl.pallas_call(write_out, out_shape=[jax.ShapeDtypeStruct((n, ROWS, cols)...  0.74 us

profile of v2, /device:TPU:100, one launch (start us, length us, event | category | flops | bytes accessed | tf_op | source)
XLA Modules:
  0.0 24.6 jit_solution(16349151239659379293)
XLA Ops:
  0.6 23.2 %shard_map.58.maps = f32[12,24,256]{2,1,0:T(8,128)S(1)} custom-call(bf16[64,48,2048]{2,1,0:T(8,128)(2,1)} %bitcast.16, s32[384,128]{1,0:T(8,128)} %bitcast.17, s32[24,256]{1,0:T(8,128)} %bitcast.18), custom_call_target="tpu_custom_call" | custom-call | tf_op jit(solution)/shard_map/pallas_call | solution.py:385
  23.8 0.7 %shard_map.59 = (f32[2,24,256]{2,1,0:T(8,128)}, f32[3,24,256]{2,1,0:T(8,128)}, f32[7,24,256]{2,1,0:T(8,128)}) custom-call(f32[12,24,256]{2,1,0:T(8,128)S(1)} %shard_map.58.maps), custom_call_target="tpu_custom_call" | custom-call | tf_op jit(solution)/shard_map/pallas_call | solution.py:416

commit v3 on v2

--- a/solution.py
+++ b/solution.py
@@ -99,9 +99,9 @@
 def kernel(
     sizes, frames, exponents, valid, out,
     buf, exp_ref, mask_ref, factor_ref, spread_ref, weight_ref, grown_ref,
-    part, early, halves, late, last, orient,
+    part, early, far, late, last, orient,
     left_halo, right_halo, up_halo, down_halo, layer_halo,
-    in_sem, small_sem, early_send, early_recv, half_send, half_recv,
+    in_sem, small_sem, early_send, early_recv, far_send, far_recv,
     late_send, late_recv, last_send, last_recv, halo_send, halo_recv,
 ):
     count, tiles = sizes
@@ -114,6 +114,7 @@
     other = (1 - px) * ring + py
     above = px * ring + lax.rem(py + 1, ring)
     below = px * ring + lax.rem(py + ring - 1, ring)
+    across = px * ring + lax.rem(py + 2, ring)
     has_next_tile = tile < tiles - 1
     has_last_tile = tile > 0
     has_next_angle = me < count - 1
@@ -123,7 +124,6 @@
 
     def owner(role):
         swap = jnp.logical_or(role < 3, role == 6)
-        shift = jnp.where(role >= 6, 0, 2)
         turn = lax.rem(role, 3)
         shift = jnp.where(role < 6, jnp.where(turn == 0, 2, jnp.where(turn == 1, 1, ring - 1)), 0)
         return jnp.where(swap, 1 - px, px) * ring + lax.rem(py + shift, ring)
@@ -148,12 +148,13 @@
     greet({"angle": other})
     greet({"angle": above})
     greet({"angle": below})
+    greet({"angle": across})
     greet({"layer": 1 - layer})
     pl.when(has_last_tile)(lambda: greet({"tile": tile - 1}))
     pl.when(has_next_tile)(lambda: greet({"tile": tile + 1}))
     pl.when(far_next)(lambda: greet({"angle": me + 1}))
     pl.when(far_last)(lambda: greet({"angle": me - 1}))
-    partners = 4
+    partners = 5
     for present in (has_last_tile, has_next_tile, far_next, far_last):
         partners = partners + present.astype(jnp.int32)
 
@@ -179,18 +180,15 @@
             early_send.at[role, g], early_recv.at[role, g], {"angle": to},
         )
 
-    def half_copy(side, g):
-        which = pl.ds(3 * side, 3)
-        return remote(
-            part.at[3, which, rows(g), :], halves.at[side, :, rows(g), :],
-            half_send.at[side, g], half_recv.at[side, g],
-            {"angle": below if side else above},
-        )
-
-    def late_copy(side, g):
-        return remote(
-            part.at[4 + side, :, rows(g), :], late.at[side, :, rows(g), :],
-            late_send.at[side, g], late_recv.at[side, g],
+    def far_copy(g):
+        return remote(
+            part.at[3, :, rows(g), :], far.at[:, rows(g), :], far_send.at[g], far_recv.at[g],
+            {"angle": across},
+        )
+
+    def late_copy(side):
+        return remote(
+            part.at[4 + side], late.at[side], late_send.at[side], late_recv.at[side],
             {"angle": below if side else above},
         )
 
@@ -220,33 +218,26 @@
             for g in ORDER:
                 early_copy(role, g).start()
 
-        @pl.when(role == 5)
-        def _():
-            for g in ORDER:
-                early_copy(0, g).wait_recv()
-                part[3, :, 8 * g : 8 * g + 8] += early[0, :, 8 * g : 8 * g + 8]
-                half_copy(0, g).start()
-                half_copy(1, g).start()
+        for side in range(2):
+
+            @pl.when(role == 4 + side)
+            def _():
+                late_copy(side).start()
 
         return carry
 
     lax.fori_loop(0, count, one, 0)
 
+    for g in ORDER:
+        early_copy(0, g).wait_recv()
+        part[3, :, 8 * g : 8 * g + 8] += early[0, :, 8 * g : 8 * g + 8]
+        far_copy(g).start()
     for g in ORDER:
         here = slice(8 * g, 8 * g + 8)
         early_copy(1, g).wait_recv()
         early_copy(2, g).wait_recv()
         part[6, :, here] += early[1, :, here] + early[2, :, here]
         last_copy(g).start()
-    for g in ORDER:
-        here = slice(8 * g, 8 * g + 8)
-        half_copy(0, g).wait_recv()
-        part[4, 0:3, here] += halves[0, :, here]
-        late_copy(0, g).start()
-        half_copy(1, g).wait_recv()
-        part[5, 3:6, here] += halves[1, :, here]
-        late_copy(1, g).start()
-
     @pl.when(jnp.logical_not(has_last_tile))
     def _():
         up_halo[...] = jnp.zeros_like(up_halo)
@@ -291,12 +282,14 @@
     )
 
     mask_copy.wait()
+    for side in range(2):
+        late_copy(side).wait_recv()
     for g in ORDER:
         here = slice(8 * g, 8 * g + 8)
-        late_copy(0, g).wait_recv()
-        late_copy(1, g).wait_recv()
+        far_copy(g).wait_recv()
         last_copy(g).wait_recv()
-        total = part[7, :, here] + (late[0, :, here] + late[1, :, here]) + last[:, here]
+        total = (part[7, :, here] + far[:, here]) + (late[0, :, here] + late[1, :, here])
+        total = total + last[:, here]
         field = [total[1] / total[0], total[2] / total[0]]
         orient[0, here] = field[0]
         orient[1, here] = field[1]
@@ -348,13 +341,13 @@
     for g in ORDER:
         for role in range(3):
             early_copy(role, g).wait_send()
-        for side in range(2):
-            half_copy(side, g).wait_send()
-            late_copy(side, g).wait_send()
+        far_copy(g).wait_send()
         last_copy(g).wait_send()
         to_layer(g).wait_send()
         pl.when(has_next_angle)(lambda: to_next_angle(g).wait_send())
         pl.when(has_last_angle)(lambda: to_last_angle(g).wait_send())
+    for side in range(2):
+        late_copy(side).wait_send()
     pl.when(has_next_tile)(lambda: to_next_tile.wait_send())
     pl.when(has_last_tile)(lambda: to_last_tile.wait_send())
 
@@ -397,7 +390,7 @@
             pltpu.VMEM((2, 96, DEPTH), bf16),
             pltpu.VMEM((count,) + block, f32),
             pltpu.VMEM((3,) + block, f32),
-            pltpu.VMEM((2, 3, ROWS, cols), f32),
+            pltpu.VMEM(block, f32),
             pltpu.VMEM((2,) + block, f32),
             pltpu.VMEM(block, f32),
             pltpu.VMEM((2, ROWS, cols), f32),
@@ -406,8 +399,8 @@
             pltpu.VMEM((2, 8, cols), f32),
             pltpu.VMEM((2, 8, cols), f32),
             pltpu.VMEM((2, ROWS, cols), f32),
-            dma((count,)), dma((2,)), dma((3, 3)), dma((3, 3)), dma((2, 3)), dma((2, 3)),
-            dma((2, 3)), dma((2, 3)), dma((3,)), dma((3,)), dma((4, 3)), dma((4, 3)),
+            dma((count,)), dma((2,)), dma((3, 3)), dma((3, 3)), dma((3,)), dma((3,)),
+            dma((2,)), dma((2,)), dma((3,)), dma((3,)), dma((4, 3)), dma((4, 3)),
         ],
         compiler_params=pltpu.CompilerParams(
             collective_id=0, has_side_effects=True, vmem_limit_bytes=52 * 1024 * 1024

time: 24.7 us -> 23.7 us (0.960); the launches traced: 24.6 us -> 23.3 us
  Pallas kernels: 23.9 us -> 22.6 us
    pallas_call x1, Pallas kernels: 23.2 us -> 21.9 us  [on_device(): pl.pallas_call(functools.partial(kernel, (count, tiles)), out_shape=jax.S...]
where the time goes in v3:
time: 23.7 us; the launch traced here: 23.3 us
  Pallas kernels  22.6 us (95%)
  between operations  0.64 us (3%)
    pallas_call x1, Pallas kernels, on_device(): pl.pallas_call(functools.partial(kernel, (count, tiles)), out_shape=jax.S...  21.9 us
    pallas_call x1, Pallas kernels, on_device(): pl.pallas_call(write_out, out_shape=[jax.ShapeDtypeStruct((n, ROWS, cols)...  0.74 us

profile of v3, /device:TPU:100, one launch (start us, length us, event | category | flops | bytes accessed | tf_op | source)
XLA Modules:
  0.0 23.3 jit_solution(9533639921597116790)
XLA Ops:
  0.6 21.9 %shard_map.58.maps = f32[12,24,256]{2,1,0:T(8,128)S(1)} custom-call(bf16[64,48,2048]{2,1,0:T(8,128)(2,1)} %bitcast.16, s32[384,128]{1,0:T(8,128)} %bitcast.17, s32[24,256]{1,0:T(8,128)} %bitcast.18), custom_call_target="tpu_custom_call" | custom-call | tf_op jit(solution)/shard_map/pallas_call | solution.py:378
  22.5 0.7 %shard_map.59 = (f32[2,24,256]{2,1,0:T(8,128)}, f32[3,24,256]{2,1,0:T(8,128)}, f32[7,24,256]{2,1,0:T(8,128)}) custom-call(f32[12,24,256]{2,1,0:T(8,128)S(1)} %shard_map.58.maps), custom_call_target="tpu_custom_call" | custom-call | tf_op jit(solution)/shard_map/pallas_call | solution.py:409

commit v4 on v3

--- a/solution.py
+++ b/solution.py
@@ -65,15 +65,15 @@
     lax.fori_loop(0, 16, one, 0)
 
 
-def grow(role, dest, factor_ref, spread_ref, grown_ref):
+def grow(step, dest, factor_ref, spread_ref, grown_ref):
     both = factor_ref[pl.ds(2 * dest, 2)].reshape(96, 2 * ANGLES_HERE)
-    grown_ref[lax.rem(role, 2)] = jnp.dot(
+    grown_ref[lax.rem(step, 2)] = jnp.dot(
         both, spread_ref[...], preferred_element_type=jnp.float32
     ).astype(jnp.bfloat16)
 
 
-def partial_moments(role, buf, grown_ref, weight_ref, part):
-    slot = lax.rem(role, 2)
+def partial_moments(step, role, buf, grown_ref, weight_ref, part):
+    slot = lax.rem(step, 2)
     for side in range(2):
         sums = []
         for kind in range(3):
@@ -128,6 +128,9 @@
         shift = jnp.where(role < 6, jnp.where(turn == 0, 2, jnp.where(turn == 1, 1, ring - 1)), 0)
         return jnp.where(swap, 1 - px, px) * ring + lax.rem(py + shift, ring)
 
+    def role_at(step):
+        return jnp.where(step < 2, 1 - step, step)
+
     def chunk(role):
         begin = pl.multiple_of(owner(role) * cols, cols)
         return pltpu.make_async_copy(
@@ -138,7 +141,7 @@
     mask_copy = pltpu.make_async_copy(valid, mask_ref, small_sem.at[1])
     exp_copy.start()
     for role in range(AHEAD):
-        chunk(jnp.int32(role)).start()
+        chunk(role_at(jnp.int32(role))).start()
 
     barrier = pltpu.get_barrier_semaphore()
 
@@ -162,7 +165,7 @@
     exp_copy.wait()
     mask_copy.start()
     fill_factors(exp_ref, factor_ref)
-    grow(jnp.int32(0), owner(jnp.int32(0)), factor_ref, spread_ref, grown_ref)
+    grow(jnp.int32(0), owner(role_at(jnp.int32(0))), factor_ref, spread_ref, grown_ref)
 
     def remote(src, dst, send, recv, where):
         return pltpu.make_async_remote_copy(
@@ -198,18 +201,19 @@
             {"angle": other},
         )
 
-    def one(role, carry):
+    def one(step, carry):
+        role = role_at(step)
         chunk(role).wait()
 
-        @pl.when(role + AHEAD < count)
+        @pl.when(step + AHEAD < count)
         def _():
-            chunk(role + AHEAD).start()
-
-        following = jnp.minimum(role + 1, count - 1)
-        grow(role + 1, owner(following), factor_ref, spread_ref, grown_ref)
-        partial_moments(role, buf, grown_ref, weight_ref, part)
-
-        @pl.when(role == 0)
+            chunk(step + AHEAD).start()
+
+        following = jnp.minimum(step + 1, count - 1)
+        grow(step + 1, owner(role_at(following)), factor_ref, spread_ref, grown_ref)
+        partial_moments(step, role, buf, grown_ref, weight_ref, part)
+
+        @pl.when(step == 0)
         def _():
             pl.semaphore_wait(barrier, partners)
 
@@ -281,7 +285,6 @@
         {"tile": tile - 1},
     )
 
-    mask_copy.wait()
     for side in range(2):
         late_copy(side).wait_recv()
     for g in ORDER:
@@ -293,19 +296,24 @@
         field = [total[1] / total[0], total[2] / total[0]]
         orient[0, here] = field[0]
         orient[1, here] = field[1]
-        to_layer(g).start()
+        part[7, :, here] = total
         pl.when(has_next_angle)(lambda: to_next_angle(g).start())
         pl.when(has_last_angle)(lambda: to_last_angle(g).start())
         if g == 0:
             pl.when(has_last_tile)(lambda: to_last_tile.start())
         if g == 2:
             pl.when(has_next_tile)(lambda: to_next_tile.start())
+        to_layer(g).start()
+    mask_copy.wait()
+    for g in ORDER:
+        here = slice(8 * g, 8 * g + 8)
         mask = mask_ref[here].astype(jnp.float32)
-        out[0, here] = field[0] * mask
-        out[1, here] = field[1] * mask
-        out[2, here] = (total[3] / total[0] - field[0] * field[0]) * mask
-        out[3, here] = (total[4] / total[0] - field[1] * field[1]) * mask
-        out[4, here] = (total[5] / total[0] - field[0] * field[1]) * mask
+        out[0, here] = orient[0, here] * mask
+        out[1, here] = orient[1, here] * mask
+        zeroth = part[7, 0, here]
+        out[2, here] = (part[7, 3, here] / zeroth - orient[0, here] * orient[0, here]) * mask
+        out[3, here] = (part[7, 4, here] / zeroth - orient[1, here] * orient[1, here]) * mask
+        out[4, here] = (part[7, 5, here] / zeroth - orient[0, here] * orient[1, here]) * mask
 
     pl.when(has_last_tile)(lambda: to_next_tile.wait_recv())
     pl.when(has_next_tile)(lambda: to_last_tile.wait_recv())

time: 23.7 us -> 23.5 us (level)
  no operation moved by 1% of the time
where the time goes in v4:
time: 23.5 us; the launch traced here: 23.1 us
  Pallas kernels  22.5 us (96%)
  between operations  0.64 us (3%)
    pallas_call x1, Pallas kernels, on_device(): pl.pallas_call(functools.partial(kernel, (count, tiles)), out_shape=jax.S...  21.7 us
    pallas_call x1, Pallas kernels, on_device(): pl.pallas_call(write_out, out_shape=[jax.ShapeDtypeStruct((n, ROWS, cols)...  0.74 us

profile of v4, /device:TPU:100, one launch (start us, length us, event | category | flops | bytes accessed | tf_op | source)
XLA Modules:
  0.0 23.1 jit_solution(206934816828324768)
XLA Ops:
  0.6 21.7 %shard_map.58.maps = f32[12,24,256]{2,1,0:T(8,128)S(1)} custom-call(bf16[64,48,2048]{2,1,0:T(8,128)(2,1)} %bitcast.16, s32[384,128]{1,0:T(8,128)} %bitcast.17, s32[24,256]{1,0:T(8,128)} %bitcast.18), custom_call_target="tpu_custom_call" | custom-call | tf_op jit(solution)/shard_map/pallas_call | solution.py:386
  22.4 0.7 %shard_map.59 = (f32[2,24,256]{2,1,0:T(8,128)}, f32[3,24,256]{2,1,0:T(8,128)}, f32[7,24,256]{2,1,0:T(8,128)}) custom-call(f32[12,24,256]{2,1,0:T(8,128)S(1)} %shard_map.58.maps), custom_call_target="tpu_custom_call" | custom-call | tf_op jit(solution)/shard_map/pallas_call | solution.py:417

commit v5 on v4

--- a/solution.py
+++ b/solution.py
@@ -228,14 +228,19 @@
             def _():
                 late_copy(side).start()
 
+        for turn, g in enumerate(ORDER):
+
+            @pl.when(step == 5 + turn)
+            def _():
+                here = slice(8 * g, 8 * g + 8)
+                early_copy(0, g).wait_recv()
+                part[3, :, here] += early[0, :, here]
+                far_copy(g).start()
+
         return carry
 
     lax.fori_loop(0, count, one, 0)
 
-    for g in ORDER:
-        early_copy(0, g).wait_recv()
-        part[3, :, 8 * g : 8 * g + 8] += early[0, :, 8 * g : 8 * g + 8]
-        far_copy(g).start()
     for g in ORDER:
         here = slice(8 * g, 8 * g + 8)
         early_copy(1, g).wait_recv()

time: 23.5 us -> 23.5 us (level)
  no operation moved by 1% of the time
where the time goes in v5:
time: 23.5 us; the launch traced here: 23.1 us
  Pallas kernels  22.5 us (96%)
  between operations  0.64 us (3%)
    pallas_call x1, Pallas kernels, on_device(): pl.pallas_call(functools.partial(kernel, (count, tiles)), out_shape=jax.S...  21.7 us
    pallas_call x1, Pallas kernels, on_device(): pl.pallas_call(write_out, out_shape=[jax.ShapeDtypeStruct((n, ROWS, cols)...  0.74 us

profile of v5, /device:TPU:100, one launch (start us, length us, event | category | flops | bytes accessed | tf_op | source)
XLA Modules:
  0.0 23.1 jit_solution(9501061497517544897)
XLA Ops:
  0.6 21.7 %shard_map.58.maps = f32[12,24,256]{2,1,0:T(8,128)S(1)} custom-call(bf16[64,48,2048]{2,1,0:T(8,128)(2,1)} %bitcast.16, s32[384,128]{1,0:T(8,128)} %bitcast.17, s32[24,256]{1,0:T(8,128)} %bitcast.18), custom_call_target="tpu_custom_call" | custom-call | tf_op jit(solution)/shard_map/pallas_call | solution.py:391
  22.4 0.7 %shard_map.59 = (f32[2,24,256]{2,1,0:T(8,128)}, f32[3,24,256]{2,1,0:T(8,128)}, f32[7,24,256]{2,1,0:T(8,128)}) custom-call(f32[12,24,256]{2,1,0:T(8,128)S(1)} %shard_map.58.maps), custom_call_target="tpu_custom_call" | custom-call | tf_op jit(solution)/shard_map/pallas_call | solution.py:422
